TPU v7x, 256 devices: a whole 4x4x8 slice. The times are simulated.
256 devices in a mesh: kx: 8 (over z_hi, x), ky: 16 (over z_lo, y), af: 2 (over core).
Axes of the slice: x: 4, y: 4, z: 8 (z_hi: 2, z_lo: 4; z = z_hi * 4 + z_lo), core: 2. Of those that a mesh axis runs over, the one named last changes fastest.
Arguments:
- vertex: float32 [2, 8, 16, 768, 768], P(None, 'kx', 'ky', 'af'), may hold values from -1.2 to 1.2
- bare_vertex: float32 [2, 8, 16, 768, 768], P(None, 'kx', 'ky', 'af'), may hold values from -1.2 to 1.2
- bubble_direct: float32 [2, 8, 16, 768], P(None, 'kx', 'ky'), may hold values from 0.1 to 1
- bubble_crossed: float32 [2, 8, 16, 768], P(None, 'kx', 'ky'), may hold values from 0.1 to 1
- shear_in: int32 [2, 768], replicated, may hold values from 0 to 15, as said below
- shear_out: int32 [2, 768], replicated, may hold values from 0 to 15, as said below
Outputs:
- updated: float32 [2, 8, 16, 768, 768], P(None, 'kx', 'ky', 'af')
Inputs may be any that keep to these rules, and one draw needn't show every extreme that they name: `shear_in`: row 0 holds each matrix row's shift of the first momentum component (below 16), row 1 that of the second (below 16). Within each half of the 768 rows, every pair (first shift mod 8, second shift) occurs for exactly 3 rows. `shear_out`: same structure as shear_in.
All inputs are finite; a program needn't handle non-finite values.
Results may differ from a plain program's by a relative error of at most 0.000082.
Values sent between devices are 32-bit elements; how exact they have to be, the bound alone decides.
A program may use at most 64 MiB of HBM per device.

v0:
```python
import jax
import jax.numpy as jnp
from jax import lax
from jax.sharding import PartitionSpec as P

mixing = 0.5


def ladder(vertex_rows, bubble_row):
    scaled = vertex_rows * bubble_row[:, None, :]
    whole = lax.all_gather(vertex_rows, "af", axis=1, tiled=True)
    return jnp.einsum(
        "hrk,hkc->hrc",
        scaled,
        whole,
        precision=lax.Precision.HIGHEST,
        preferred_element_type=jnp.float32,
    )


def pack_rows(data, target):
    row_order = jnp.argsort(target, stable=True)
    return jnp.take(data, row_order, axis=1)


def unpack_rows(data, anchor):
    row_order = jnp.argsort(anchor, stable=True)
    inverse = jnp.argsort(row_order, stable=True)
    return jnp.take(data, inverse, axis=1)


def crossing(vertex_rows, shear_table):
    item_count = vertex_rows.shape[0]
    row_count = vertex_rows.shape[1]
    row_first = lax.axis_index("af") * row_count
    shift_x = lax.dynamic_slice_in_dim(shear_table[0], row_first, row_count)
    shift_y = lax.dynamic_slice_in_dim(shear_table[1], row_first, row_count)
    width_x = lax.axis_size("kx")
    width_y = lax.axis_size("ky")
    kx_index = lax.axis_index("kx")
    ky_index = lax.axis_index("ky")
    carry_bit = (kx_index + shift_x % width_x >= width_x).astype(jnp.int32)
    item_turn = (shift_x // width_x + carry_bit) % item_count
    turned = vertex_rows
    rolled = jnp.roll(vertex_rows, 1, axis=0)
    turned = jnp.where((item_turn == 1)[None, :, None], rolled, turned)
    target_x = (kx_index + shift_x) % width_x
    target_y = (ky_index + shift_y) % width_y
    anchor_x = (kx_index - shift_x) % width_x
    anchor_y = (ky_index - shift_y) % width_y
    arrived = lax.all_to_all(
        pack_rows(turned, target_x * width_y + target_y),
        ("kx", "ky"),
        split_axis=1,
        concat_axis=1,
        tiled=True,
    )
    return unpack_rows(arrived, anchor_x * width_y + anchor_y)


def body(vertex, bare_vertex, bubble_direct, bubble_crossed, shear_in, shear_out):
    item_count = vertex.shape[0]
    row_count = vertex.shape[3]
    columns = vertex.shape[4]
    local_field = vertex.reshape(item_count, row_count, columns)
    local_bare = bare_vertex.reshape(item_count, row_count, columns)
    direct_bubble = bubble_direct.reshape(item_count, columns)
    crossed_bubble = bubble_crossed.reshape(item_count, columns)
    direct_ladder = ladder(local_field, direct_bubble)
    crossed = crossing(local_field, shear_in)
    crossed_ladder = ladder(crossed, crossed_bubble)
    returned = crossing(crossed_ladder, shear_out)
    updated = (1.0 - mixing) * local_field + mixing * (local_bare + direct_ladder + returned)
    return updated.reshape(vertex.shape)


def solution(mesh):
    placed = (
        P(None, "kx", "ky", "af", None),
        P(None, "kx", "ky", "af", None),
        P(None, "kx", "ky", None),
        P(None, "kx", "ky", None),
        P(),
        P(),
    )
    return jax.shard_map(
        body, mesh=mesh, in_specs=placed, out_specs=P(None, "kx", "ky", "af", None), check_vma=False
    )
```

profile of v0, /device:TPU:6, one launch (start us, length us, event | category | flops | bytes accessed | tf_op | source)
XLA Modules:
  0.0 235.8 jit_solution(4095748847329514280)
XLA Ops:
  6.5 0.8 fusion.44
  7.4 3.8 %sort.87 = (s32[384]{0:T(512)}, s32[384]{0:T(512)S(1)}) sort(s32[384]{0:T(512)S(1)} %get-tuple-element.33, s32[384]{0:T(512)S(1)} %iota.19), dimensions={0}, to_apply=%region_0.1 | sort | flops 3456 | bytes 6144 | tf_op jit(solution)/shard_map/jit(argsort)/sort | solution.py:22
  11.2 1.9 slice_bitcast_fusion.1
  13.1 0.4 copy-done
  13.6 0.5 maximum_select_fusion
  14.1 3.2 %copy.10 = f32[2,384,768]{2,0,1:T(2,128)} copy(f32[2,384,768]{2,1,0:T(8,128)S(1)} %maximum_select_fusion) | data formatting | bytes 4718592 | tf_op jit(solution)/shard_map/jit(_where)/select_n | solution.py:46
  17.3 5.1 %gather_fusion = f32[384,2,768]{2,1,0:T(2,128)S(1)} fusion(f32[2,384,768]{2,0,1:T(2,128)} %copy.10, s32[1024]{0:T(1024)S(1)} %pad_clamp_fusion.3), kind=kCustom, calls=%fused_computation.clone | custom fusion | bytes 4720128 | tf_op jit(solution)/shard_map/jit(_take)/gather | solution.py:23
  22.4 2.8 %select_bitcast_fusion.1 = f32[2,384,768]{2,0,1:T(2,128)} fusion(f32[384,2,768]{2,1,0:T(2,128)S(1)} %gather_fusion, pred[384]{0:T(512)(128)(4,1)S(1)} %compare_and_fusion.3), kind=kLoop, calls=%fused_computation.18 | loop fusion | flops 589824 | bytes 4718976 | tf_op jit(solution)/shard_map/jit(_take)/select_n | solution.py:23
  25.1 15.6 %all-to-all-start = ((f32[2,384,768]{2,0,1:T(2,128)}), f32[2,384,768]{2,0,1:T(2,128)S(1)}, u32[]{:S(2)}, u32[]{:S(2)}) async-start(f32[2,384,768]{2,0,1:T(2,128)} %select_bitcast_fusion.1), calls=%async_computation | async-start | bytes 4718592 | tf_op jit(solution)/shard_map/all_to_all | solution.py:51
  40.7 0.0 all-gather.4.cloned.1.call-start
  40.8 3.8 %sort.88 = (s32[384]{0:T(512)}, s32[384]{0:T(512)S(1)}) sort(s32[384]{0:T(512)S(1)} %get-tuple-element.32, s32[384]{0:T(512)S(1)} %iota.20), dimensions={0}, to_apply=%region_1.3 | sort | flops 3456 | bytes 6144 | tf_op jit(solution)/shard_map/jit(argsort)/sort | solution.py:27
  44.6 3.8 %sort.89 = (s32[384]{0:T(512)}, s32[384]{0:T(512)S(1)}) sort(s32[384]{0:T(512)S(1)} %get-tuple-element.13, s32[384]{0:T(512)S(1)} %iota.21), dimensions={0}, to_apply=%region_2.4 | sort | flops 3456 | bytes 6144 | tf_op jit(solution)/shard_map/jit(argsort)/sort | solution.py:28
  48.4 47.8 %all-to-all-done = f32[2,384,768]{2,0,1:T(2,128)S(1)} async-done(((f32[2,384,768]{2,0,1:T(2,128)}), f32[2,384,768]{2,0,1:T(2,128)S(1)}, u32[]{:S(2)}, u32[]{:S(2)}) %all-to-all-start) | async-done | bytes 2359328 | tf_op jit(solution)/shard_map/all_to_all | solution.py:51
  96.1 5.2 %gather_fusion.1 = f32[384,2,768]{2,1,0:T(2,128)} fusion(f32[2,384,768]{2,0,1:T(2,128)S(1)} %all-to-all-done, s32[1024]{0:T(1024)S(1)} %pad_clamp_fusion.2), kind=kCustom, calls=%fused_computation.1.clone | custom fusion | bytes 4720128 | tf_op jit(solution)/shard_map/jit(_take)/gather | solution.py:29
  101.3 3.3 %fusion.5 = f32[2,384,768]{2,1,0:T(8,128)} fusion(f32[384,2,768]{2,1,0:T(2,128)} %gather_fusion.1, pred[384]{0:T(512)(128)(4,1)S(1)} %compare_and_fusion.2), kind=kLoop, calls=%fused_computation.16 | loop fusion | flops 589824 | bytes 4718976 | tf_op jit(solution)/shard_map/jit(_take)/select_n | solution.py:29
  104.7 0.0 all-gather.4.cloned.1.call-update
  104.7 0.2 all-gather.6.cloned.1.call-start
  104.9 0.5 all-gather.6.cloned.1.call-update
  105.6 3.8 %sort.90 = (s32[384]{0:T(512)}, s32[384]{0:T(512)S(1)}) sort(s32[384]{0:T(512)S(1)} %get-tuple-element.31, s32[384]{0:T(512)S(1)} %iota.22), dimensions={0}, to_apply=%region_3.5 | sort | flops 3456 | bytes 6144 | tf_op jit(solution)/shard_map/jit(argsort)/sort | solution.py:22
  109.4 12.5 %all-gather.4.cloned.1.call-done = f32[2,768,768]{2,1,0:T(8,128)} async-done(((f32[2,384,768]{2,1,0:T(8,128)}), f32[2,768,768]{2,1,0:T(8,128)}) %all-gather.4.cloned.1.call-update) | async-done | bytes 4718608 | tf_op jit(solution)/shard_map/all_gather | solution.py:11
  121.9 7.9 %fusion.6 = f32[2,384,768]{2,1,0:T(8,128)S(1)} fusion(f32[2,768,768]{2,1,0:T(8,128)} %all-gather.4.cloned.1.call-done, f32[2,384,768]{2,1,0:T(8,128)S(1)} %copy-done.2, f32[2,768]{1,0:T(2,128)S(1)} %bitcast.48), kind=kOutput, calls=%fused_computation.19 | convolution fusion | flops 5436407808 | bytes 9443328 | tf_op jit(solution)/shard_map/hrk,hkc->hrc/dot_general | solution.py:12
  129.8 0.2 fusion.42
  130.0 0.5 maximum_select_fusion.1
  130.5 3.2 %copy.12 = f32[2,384,768]{2,0,1:T(2,128)} copy(f32[2,384,768]{2,1,0:T(8,128)S(1)} %maximum_select_fusion.1) | data formatting | bytes 4718592 | tf_op jit(solution)/shard_map/jit(_where)/select_n | solution.py:46
  133.7 5.1 %gather_fusion.2 = f32[384,2,768]{2,1,0:T(2,128)S(1)} fusion(f32[2,384,768]{2,0,1:T(2,128)} %copy.12, s32[1024]{0:T(1024)S(1)} %pad_clamp_fusion.1), kind=kCustom, calls=%fused_computation.2.clone | custom fusion | bytes 4720128 | tf_op jit(solution)/shard_map/jit(_take)/gather | solution.py:23
  138.8 2.8 %select_bitcast_fusion = f32[2,384,768]{2,0,1:T(2,128)} fusion(f32[384,2,768]{2,1,0:T(2,128)S(1)} %gather_fusion.2, pred[384]{0:T(512)(128)(4,1)S(1)} %compare_and_fusion.1), kind=kLoop, calls=%fused_computation.17 | loop fusion | flops 589824 | bytes 4718976 | tf_op jit(solution)/shard_map/jit(_take)/select_n | solution.py:23
  141.6 14.5 %all-to-all-start.1 = ((f32[2,384,768]{2,0,1:T(2,128)}), f32[2,384,768]{2,0,1:T(2,128)}, u32[]{:S(2)}, u32[]{:S(2)}) async-start(f32[2,384,768]{2,0,1:T(2,128)} %select_bitcast_fusion), calls=%async_computation.1 | async-start | bytes 4718592 | tf_op jit(solution)/shard_map/all_to_all | solution.py:51
  156.1 3.8 %sort.91 = (s32[384]{0:T(512)}, s32[384]{0:T(512)S(1)}) sort(s32[384]{0:T(512)S(1)} %get-tuple-element.30, s32[384]{0:T(512)S(1)} %iota.23), dimensions={0}, to_apply=%region_4.6 | sort | flops 3456 | bytes 6144 | tf_op jit(solution)/shard_map/jit(argsort)/sort | solution.py:27
  159.9 3.8 %sort.92 = (s32[384]{0:T(512)}, s32[384]{0:T(512)S(1)}) sort(s32[384]{0:T(512)S(1)} %get-tuple-element.16, s32[384]{0:T(512)S(1)} %iota.24), dimensions={0}, to_apply=%region_5.7 | sort | flops 3456 | bytes 6144 | tf_op jit(solution)/shard_map/jit(argsort)/sort | solution.py:28
  163.7 47.9 %all-to-all-done.1 = f32[2,384,768]{2,0,1:T(2,128)} async-done(((f32[2,384,768]{2,0,1:T(2,128)}), f32[2,384,768]{2,0,1:T(2,128)}, u32[]{:S(2)}, u32[]{:S(2)}) %all-to-all-start.1) | async-done | bytes 2359328 | tf_op jit(solution)/shard_map/all_to_all | solution.py:51
  211.7 6.3 %gather_fusion.3 = f32[384,2,768]{2,1,0:T(2,128)} fusion(f32[2,384,768]{2,0,1:T(2,128)} %all-to-all-done.1, s32[1024]{0:T(1024)S(1)} %pad_clamp_fusion), kind=kCustom, calls=%fused_computation.3.clone | custom fusion | bytes 4720128 | tf_op jit(solution)/shard_map/jit(_take)/gather | solution.py:29
  217.9 11.0 %fusion.4 = f32[2,1,1,384,768]{4,3,2,1,0:T(8,128)} fusion(f32[2,1,1,384,768]{4,3,2,1,0:T(8,128)} %param.9, f32[2,1,1,384,768]{4,3,2,1,0:T(8,128)S(1)} %copy-done.1, f32[384,2,768]{2,1,0:T(2,128)} %gather_fusion.3, f32[2,1,1,768,768]{4,3,0,2,1:T(8,128)} %all-gather.6.cloned.1.call-done, f32[2,768]{1,0:T(2,128)S(1)} %bitcast.47, ...), kind=kOutput, calls=%fused_computation.11 | convolution fusion | flops 5439356928 | bytes 14162304 | tf_op jit(solution)/shard_map/hrk,hkc->hrc/dot_general | solution.py:12
  (40 shorter events, 0.3 us)
Async XLA Ops:
  11.2 2.4 %copy-start = (f32[2,1,1,384,768]{4,3,2,1,0:T(8,128)S(1)}, f32[2,1,1,384,768]{4,3,2,1,0:T(8,128)}, u32[]{:S(2)}) copy-start(f32[2,1,1,384,768]{4,3,2,1,0:T(8,128)} %param.8) | copy-start | bytes 7077892
  25.1 71.0 %all-to-all-start = ((f32[2,384,768]{2,0,1:T(2,128)}), f32[2,384,768]{2,0,1:T(2,128)S(1)}, u32[]{:S(2)}, u32[]{:S(2)}) async-start(f32[2,384,768]{2,0,1:T(2,128)} %select_bitcast_fusion.1), calls=%async_computation | async-start | bytes 4718592 | tf_op jit(solution)/shard_map/all_to_all | solution.py:51
  40.7 81.2 %all-gather.4.cloned.1.call-start = ((), (), s32[]{:S(2)}) async-start(), calls=%async_computation.2 | async-start | bytes 7077888 | tf_op jit(solution)/shard_map/all_gather | solution.py:11
  104.7 0.8 copy-start.3
  104.7 4.7 %copy-start.4 = (f32[2,1,1,768]{3,2,1,0:T(1,128)S(1)}, f32[2,1,1,768]{3,2,1,0:T(1,128)}, u32[]{:S(2)}) copy-start(f32[2,1,1,768]{3,2,1,0:T(1,128)} %param.11) | copy-start | bytes 18436
  104.7 17.3 %copy-start.2 = (f32[2,384,768]{2,1,0:T(8,128)S(1)}, f32[2,384,768]{2,1,0:T(8,128)}, u32[]{:S(2)}) copy-start(f32[2,384,768]{2,1,0:T(8,128)} %fusion.5) | copy-start | bytes 7077892
  104.7 113.3 %all-gather.6.cloned.1.call-start = ((), (), s32[]{:S(2)}) async-start(), calls=%async_computation.3 | async-start | bytes 7077888 | tf_op jit(solution)/shard_map/all_gather | solution.py:11
  141.5 14.5 %copy-start.5 = (f32[2,1,1,768]{3,2,1,0:T(1,128)S(1)}, f32[2,1,1,768]{3,2,1,0:T(1,128)}, u32[]{:S(2)}) copy-start(f32[2,1,1,768]{3,2,1,0:T(1,128)} %param.10) | copy-start | bytes 18436
  141.6 70.1 %all-to-all-start.1 = ((f32[2,384,768]{2,0,1:T(2,128)}), f32[2,384,768]{2,0,1:T(2,128)}, u32[]{:S(2)}, u32[]{:S(2)}) async-start(f32[2,384,768]{2,0,1:T(2,128)} %select_bitcast_fusion), calls=%async_computation.1 | async-start | bytes 4718592 | tf_op jit(solution)/shard_map/all_to_all | solution.py:51
  163.7 54.2 %copy-start.1 = (f32[2,1,1,384,768]{4,3,2,1,0:T(8,128)S(1)}, f32[2,1,1,384,768]{4,3,2,1,0:T(8,128)}, u32[]{:S(2)}) copy-start(f32[2,1,1,384,768]{4,3,2,1,0:T(8,128)} %param.8) | copy-start | bytes 7077892
Sparse Core Ops, SparseCore 0:
  104.8 17.0 all-gather.3
  123.7 21.0 all-gather.5
where the time goes:
time: 240 us; the launch traced here: 236 us
  waiting for transfers between devices  109 us (45%)
  other arithmetic  32.7 us (14%)
  local copies, waits for them, and re-layouts  31.4 us (13%)
  starting transfers between devices  30.4 us (13%)
  matrix products  18.9 us (8%)
  between operations  13.6 us (6%)
    all_to_all x2, waiting for transfers between devices, crossing(): lax.all_to_all(pack_rows(turned, target_x * width_y + target_y), ('kx', '...  95.7 us
    all_to_all x2, starting transfers between devices, crossing(): lax.all_to_all(pack_rows(turned, target_x * width_y + target_y), ('kx', '...  30.1 us
    dot_general x2, matrix products, ladder(): jnp.einsum('hrk,hkc->hrc', scaled, whole, precision=lax.Precision.HIGHEST...  18.9 us
    all_gather x2, waiting for transfers between devices, ladder(): whole = lax.all_gather(vertex_rows, 'af', axis=1, tiled=True)  12.5 us
    gather x2, local copies, waits for them, and re-layouts, unpack_rows(): return jnp.take(data, inverse, axis=1)  11.5 us
    gather x2, local copies, waits for them, and re-layouts, pack_rows(): return jnp.take(data, row_order, axis=1)  10.1 us
    sort x2, other arithmetic, unpack_rows(): inverse = jnp.argsort(row_order, stable=True)  7.57 us
    sort x2, other arithmetic, unpack_rows(): row_order = jnp.argsort(anchor, stable=True)  7.57 us
  transfers between devices with their start and end apart: 4, of which 3 were waited for; matrix products, arithmetic and copies ran while one was open for 19% of the time, Pallas kernels for 0%

commit v1 on v0

v1 whole, which is shorter than its diff:
```python
import functools

import jax
import jax.numpy as jnp
from jax import lax
from jax.experimental import pallas as pl
from jax.experimental.pallas import tpu as pltpu
from jax.sharding import PartitionSpec as P

MESH = pl.DeviceIdType.MESH
mixing = 0.5
LANES = 128
NX, NY, NZ = 4, 4, 8
CLASSES_X, CLASSES_Y = 8, 16
CLASSES = CLASSES_X * CLASSES_Y


def halves(value):
    high = value.astype(jnp.bfloat16)
    low = (value - high.astype(jnp.float32)).astype(jnp.bfloat16)
    return high, low


def product(left, right):
    return jnp.dot(left, right, preferred_element_type=jnp.float32)


def column_of(row):
    wide = jnp.broadcast_to(row, (8, row.shape[1])).astype(jnp.float32)
    return wide.T[:, :1].astype(jnp.int32)


def tables(shear, first, rows):
    shift_x = shear[0:1, pl.ds(first, rows)]
    shift_y = shear[1:2, pl.ds(first, rows)]
    group_row = (shift_x & (CLASSES_X - 1)) * CLASSES_Y + shift_y
    group_col = column_of(group_row)
    high_col = column_of(shift_x) // CLASSES_X
    along0 = lax.broadcasted_iota(jnp.int32, (rows, rows), 0)
    along1 = lax.broadcasted_iota(jnp.int32, (rows, rows), 1)
    same = group_row == group_col
    each = rows // CLASSES
    rank_row = jnp.sum(jnp.where(same & (along0 < along1), 1.0, 0.0), axis=0, keepdims=True).astype(jnp.int32)
    rank_col = jnp.sum(jnp.where(same & (along1 < along0), 1.0, 0.0), axis=1, keepdims=True).astype(jnp.int32)
    pack = jnp.where(along0 == group_row * each + rank_row, 1.0, 0.0).astype(jnp.bfloat16)
    unpack = jnp.where(along1 == group_col * each + rank_col, 1.0, 0.0).astype(jnp.bfloat16)
    return group_col // CLASSES_Y, high_col, pack, unpack


def kernel(
    v_hbm, b_hbm, c1, c2, shear_in, shear_out, out_hbm,
    v, vp, acc, pk0, pk1, rv0, rv1, rp0, rp1, ok0, ok1, or0, or1,
    lh, ll, rights, p_in, u_own, u_other, q_mix, u_out, turn_in, turn_out,
    load_sem, store_sem, pair_send, pair_recv, in_send, in_recv, out_send, out_recv,
):
    rows, columns = v.shape[1:]
    strips = columns // LANES
    piece = rows // CLASSES * strips
    lines = rows * strips
    kx, ky, af = lax.axis_index("kx"), lax.axis_index("ky"), lax.axis_index("af")
    x, y, z = kx % NX, ky % NY, (kx // NX) * (NZ // 2) + ky // NY
    own = pl.multiple_of(af * rows, rows)
    other = pl.multiple_of((1 - af) * rows, rows)
    partner = (kx, ky, 1 - af)

    def place(step):
        tx, ty, tz = (x + step // (NY * NZ)) % NX, (y + step // NZ % NY) % NY, (z + step % NZ) % NZ
        return (tz // (NZ // 2)) * NX + tx, (tz % (NZ // 2)) * NY + ty

    loads = [pltpu.make_async_copy(v_hbm, v, load_sem.at[0]), pltpu.make_async_copy(b_hbm, acc, load_sem.at[1])]
    for load in loads:
        load.start()

    barrier = pltpu.get_barrier_semaphore()

    def greet(step, carry):
        tx, ty = place(step)
        pl.semaphore_signal(barrier, inc=1, device_id=(tx, ty, af), device_id_type=MESH)
        return carry

    lax.fori_loop(1, CLASSES, greet, 0)
    pl.semaphore_signal(barrier, inc=1, device_id=partner, device_id_type=MESH)

    class_col, high_col, pack, unpack = tables(shear_in, own, rows)
    p_in[...] = pack
    u_own[...] = unpack
    turn_in[...] = (high_col + (class_col + kx >= CLASSES_X).astype(jnp.int32)) & 1
    loads[0].wait()

    def pack_item(item, into):
        for tile in range(columns // 256):
            span = slice(tile * 256, tile * 256 + 256)
            field = jnp.where(turn_in[...] == 1, v[1 - item, :, span], v[item, :, span])
            high, low = halves(field)
            packed = product(p_in[...], high) + product(p_in[...], low)
            for half in range(2):
                into[pl.ds(2 * tile + half, rows, stride=strips), :] = packed[:, half * LANES : half * LANES + LANES]

    def send_item(source, target, send_sem, recv_sem):
        def send(step, carry):
            tx, ty = place(step)
            group = ((tx + CLASSES_X - kx) % CLASSES_X) * CLASSES_Y + (ty + CLASSES_Y - ky) % CLASSES_Y
            part = pl.ds(group * piece, piece)
            pltpu.make_async_remote_copy(
                src_ref=source.at[part],
                dst_ref=target.at[part],
                send_sem=send_sem,
                recv_sem=recv_sem,
                device_id=(tx, ty, af),
                device_id_type=MESH,
            ).start()
            return carry

        lax.fori_loop(1, CLASSES, send, 0)
        target[0:piece, :] = source[0:piece, :]

    def wait_item(buffer, sem):
        part = buffer.at[pl.ds(piece, lines - piece)]
        pltpu.make_async_copy(part, part, sem).wait()

    def to_partner(source, target, place_of):
        return pltpu.make_async_remote_copy(
            src_ref=source,
            dst_ref=target,
            send_sem=pair_send.at[place_of],
            recv_sem=pair_recv.at[place_of],
            device_id=partner,
            device_id_type=MESH,
        )

    def plain(buffer):
        parts = [halves(buffer[pl.ds(strip, rows, stride=strips), :]) for strip in range(strips)]
        return jnp.concatenate([p[0] for p in parts], axis=1), jnp.concatenate([p[1] for p in parts], axis=1)

    def ladder(tile, rh, rl):
        span = slice(tile * 256, tile * 256 + 256)
        return product(lh[...], rh[:, span]) + product(ll[...], rh[:, span]) + product(lh[...], rl[:, span])

    pack_item(0, pk0)
    pl.semaphore_wait(barrier, CLASSES)

    field_copy = to_partner(v, vp, 0)
    field_copy.start()
    send_item(pk0, rv0, in_send.at[0], in_recv.at[0])
    pack_item(1, pk1)
    send_item(pk1, rv1, in_send.at[1], in_recv.at[1])

    u_other[...] = tables(shear_in, other, rows)[3]
    class_col, high_col, pack, unpack = tables(shear_out, own, rows)
    turn_out[...] = (high_col + (class_col > kx).astype(jnp.int32)) & 1
    u_out[...] = unpack
    q_mix[...] = product(pack, u_own[...]).astype(jnp.bfloat16)

    loads[1].wait()
    field_copy.wait()
    for item in range(2):
        rh, rl = rights.at[0, item], rights.at[1, item]
        rh[pl.ds(own, rows), :], rl[pl.ds(own, rows), :] = halves(v[item])
        rh[pl.ds(other, rows), :], rl[pl.ds(other, rows), :] = halves(vp[item])
        lh[...], ll[...] = halves(v[item] * c1[item : item + 1, :])
        for tile in range(columns // 256):
            span = slice(tile * 256, tile * 256 + 256)
            acc[item, :, span] = (1.0 - mixing) * v[item, :, span] + mixing * (acc[item, :, span] + ladder(tile, rh, rl))

    def crossed_item(item, arrived, arrived_pair, into):
        rh, rl = rights.at[0, 2 + item], rights.at[1, 2 + item]
        wait_item(arrived, in_recv.at[item])
        copy = to_partner(arrived, arrived_pair, 1 + item)
        copy.start()
        high, low = plain(arrived)
        rh[pl.ds(own, rows), :] = product(u_own[...], high).astype(jnp.bfloat16)
        rl[pl.ds(own, rows), :] = product(u_own[...], low).astype(jnp.bfloat16)
        left = product(q_mix[...], high) + product(q_mix[...], low)
        lh[...], ll[...] = halves(left * c2[item : item + 1, :])
        copy.wait()
        high, low = plain(arrived_pair)
        rh[pl.ds(other, rows), :] = product(u_other[...], high).astype(jnp.bfloat16)
        rl[pl.ds(other, rows), :] = product(u_other[...], low).astype(jnp.bfloat16)
        for tile in range(columns // 256):
            term = ladder(tile, rh, rl)
            for half in range(2):
                into[pl.ds(2 * tile + half, rows, stride=strips), :] = term[:, half * LANES : half * LANES + LANES]

    crossed_item(0, rv0, rp0, ok0)
    send_item(ok0, or0, out_send.at[0], out_recv.at[0])
    crossed_item(1, rv1, rp1, ok1)
    send_item(ok1, or1, out_send.at[1], out_recv.at[1])

    def returned_item(item, arrived):
        wait_item(arrived, out_recv.at[item])
        high, low = plain(arrived)
        term = mixing * (product(u_out[...], high) + product(u_out[...], low))
        turned = turn_out[...] == 1
        acc[item] += jnp.where(turned, 0.0, term)
        acc[1 - item] += jnp.where(turned, term, 0.0)

    returned_item(0, or0)
    returned_item(1, or1)
    store = pltpu.make_async_copy(acc, out_hbm, store_sem)
    store.start()
    for item, (first, second) in enumerate(((pk0, ok0), (pk1, ok1))):
        wait_item(first, in_send.at[item])
        wait_item(second, out_send.at[item])
    store.wait()


def body(vertex, bare_vertex, bubble_direct, bubble_crossed, shear_in, shear_out):
    items, _, _, rows, columns = vertex.shape
    shape = (items, rows, columns)
    lines = (rows * columns // LANES, LANES)
    vmem = pl.BlockSpec(memory_space=pltpu.VMEM)
    anywhere = pl.BlockSpec(memory_space=pl.ANY)
    wide, real = jnp.float32, jnp.bfloat16
    dma = pltpu.SemaphoreType.DMA
    updated = pl.pallas_call(
        kernel,
        out_shape=jax.ShapeDtypeStruct(shape, wide),
        in_specs=[anywhere, anywhere, vmem, vmem, vmem, vmem],
        out_specs=anywhere,
        scratch_shapes=[pltpu.VMEM(shape, wide)] * 3
        + [pltpu.VMEM(lines, wide)] * 10
        + [pltpu.VMEM((rows, columns), real)] * 2
        + [pltpu.VMEM((2, 4, columns, columns), real)]
        + [pltpu.VMEM((rows, rows), real)] * 5
        + [pltpu.VMEM((rows, 1), jnp.int32)] * 2
        + [dma((2,)), dma, dma((3,)), dma((3,)), dma((2,)), dma((2,)), dma((2,)), dma((2,))],
        compiler_params=pltpu.CompilerParams(
            collective_id=0, has_side_effects=True, vmem_limit_bytes=56 * 2**20
        ),
    )(
        vertex.reshape(shape),
        bare_vertex.reshape(shape),
        bubble_direct.reshape(items, columns),
        bubble_crossed.reshape(items, columns),
        shear_in,
        shear_out,
    )
    return updated.reshape(vertex.shape)


def solution(mesh):
    placed = (
        P(None, "kx", "ky", "af", None),
        P(None, "kx", "ky", "af", None),
        P(None, "kx", "ky", None),
        P(None, "kx", "ky", None),
        P(),
        P(),
    )
    return jax.shard_map(
        body, mesh=mesh, in_specs=placed, out_specs=P(None, "kx", "ky", "af", None), check_vma=False
    )
```

time: 240 us -> 127 us (0.53); the launches traced: 236 us -> 126 us
  Pallas kernels: 0 us -> 121 us
  waiting for transfers between devices: 109 us -> 0 us
  other arithmetic: 32.7 us -> 0 us
  starting transfers between devices: 30.4 us -> 0 us
  local copies, waits for them, and re-layouts: 31.4 us -> 4.53 us
  matrix products: 18.9 us -> 0 us
  between operations: 13.6 us -> 0.01 us
    pallas_call x0 -> x1, Pallas kernels: none -> 121 us  [body(): pl.pallas_call(kernel, out_shape=jax.ShapeDtypeStruct(shape, wide), in_sp...]
    all_to_all x2 -> x0, waiting for transfers between devices: 95.7 us -> none  [crossing(): lax.all_to_all(pack_rows(turned, target_x * width_y + target_y), ('kx', '...]
    all_to_all x2 -> x0, starting transfers between devices: 30.1 us -> none  [crossing(): lax.all_to_all(pack_rows(turned, target_x * width_y + target_y), ('kx', '...]
    sort x6 -> x0, other arithmetic: 22.7 us -> none  [the longest x2 7.57 us: unpack_rows(): inverse = jnp.argsort(row_order, stable=True)]
    gather x4 -> x0, local copies, waits for them, and re-layouts: 21.6 us -> none  [the longest x2 11.5 us: unpack_rows(): return jnp.take(data, inverse, axis=1)]
    dot_general x2 -> x0, matrix products: 18.9 us -> none  [ladder(): jnp.einsum('hrk,hkc->hrc', scaled, whole, precision=lax.Precision.HIGHEST...]
    all_gather x2 -> x0, waiting for transfers between devices: 12.5 us -> none  [ladder(): whole = lax.all_gather(vertex_rows, 'af', axis=1, tiled=True)]
    select_n x9 -> x0, other arithmetic: 9.85 us -> none  [the longest x4 5.53 us: pack_rows(): return jnp.take(data, row_order, axis=1)]
  transfers between devices with their start and end apart: 4 -> 0, of which waited for: 3 -> 0; matrix products, arithmetic and copies ran while one was open for 19% -> 0% of each run, Pallas kernels for 0% -> 0%
where the time goes in v1:
time: 127 us; the launch traced here: 126 us
  Pallas kernels  121 us (95%)
  local copies, waits for them, and re-layouts  4.53 us (4%)
    pallas_call x1, Pallas kernels, body(): pl.pallas_call(kernel, out_shape=jax.ShapeDtypeStruct(shape, wide), in_sp...  121 us
    unnamed x2, local copies, waits for them, and re-layouts  4.53 us

profile of v1, /device:TPU:6, one launch (start us, length us, event | category | flops | bytes accessed | tf_op | source)
XLA Modules:
  0.0 126.0 jit_solution(13167086927415877171)
XLA Ops:
  0.0 1.3 %copy_bitcast_fusion = (f32[2,768]{1,0:T(2,128)}, f32[2,768]{1,0:T(2,128)}) fusion(f32[2,1,1,768]{3,2,1,0:T(1,128)} %param.9, f32[2,1,1,768]{3,2,1,0:T(1,128)} %param.8), kind=kLoop, calls=%fused_computation | loop fusion | bytes 24576
  1.3 121.5 %shard_map.64 = f32[2,384,768]{2,1,0:T(8,128)} custom-call(f32[2,384,768]{2,1,0:T(8,128)} %bitcast.10, f32[2,384,768]{2,1,0:T(8,128)} %bitcast.11, f32[2,768]{1,0:T(2,128)} %get-tuple-element.6.c1, f32[2,768]{1,0:T(2,128)} %get-tuple-element.5.c2, s32[2,768]{1,0:T(2,128)} %shear_in.1, s32[2,768]{1,0:T(2,128)} %shear_out.1), custom_call_target="tpu_custom_call" | custom-call | tf_op jit(solution)/shard_map/pallas_call | solution.py:215
  122.8 3.2 %copy.13 = f32[2,1,1,384,768]{4,3,2,1,0:T(8,128)} copy(f32[2,1,1,384,768]{4,3,2,1,0:T(8,128)} %bitcast.9) | data formatting | bytes 4718592

commit v2 on v1

--- a/solution.py
+++ b/solution.py
@@ -48,9 +48,9 @@
 
 
 def kernel(
-    v_hbm, b_hbm, c1, c2, shear_in, shear_out, out_hbm,
-    v, vp, acc, pk0, pk1, rv0, rv1, rp0, rp1, ok0, ok1, or0, or1,
-    lh, ll, rights, p_in, u_own, u_other, q_mix, u_out, turn_in, turn_out,
+    v_hbm, b_hbm, c1, c2, shear_in, shear_out, acc_hbm, or1, u_out, turn_out,
+    v, vp, acc, pk0, pk1, rv0, rv1, rp0, rp1, ok0, ok1, or0,
+    lh, ll, rights, p_in, u_own, u_other, q_mix, turn_in,
     load_sem, store_sem, pair_send, pair_recv, in_send, in_recv, out_send, out_recv,
 ):
     rows, columns = v.shape[1:]
@@ -58,14 +58,14 @@
     piece = rows // CLASSES * strips
     lines = rows * strips
     kx, ky, af = lax.axis_index("kx"), lax.axis_index("ky"), lax.axis_index("af")
-    x, y, z = kx % NX, ky % NY, (kx // NX) * (NZ // 2) + ky // NY
+    x, y, z = kx & 3, ky & 3, (kx >> 2) * 4 + (ky >> 2)
     own = pl.multiple_of(af * rows, rows)
     other = pl.multiple_of((1 - af) * rows, rows)
     partner = (kx, ky, 1 - af)
 
     def place(step):
-        tx, ty, tz = (x + step // (NY * NZ)) % NX, (y + step // NZ % NY) % NY, (z + step % NZ) % NZ
-        return (tz // (NZ // 2)) * NX + tx, (tz % (NZ // 2)) * NY + ty
+        tx, ty, tz = (x + (step >> 5)) & 3, (y + (step >> 3)) & 3, (z + step) & 7
+        return (tz >> 2) * NX + tx, (tz & 3) * NY + ty
 
     loads = [pltpu.make_async_copy(v_hbm, v, load_sem.at[0]), pltpu.make_async_copy(b_hbm, acc, load_sem.at[1])]
     for load in loads:
@@ -99,7 +99,7 @@
     def send_item(source, target, send_sem, recv_sem):
         def send(step, carry):
             tx, ty = place(step)
-            group = ((tx + CLASSES_X - kx) % CLASSES_X) * CLASSES_Y + (ty + CLASSES_Y - ky) % CLASSES_Y
+            group = ((tx - kx) & (CLASSES_X - 1)) * CLASSES_Y + ((ty - ky) & (CLASSES_Y - 1))
             part = pl.ds(group * piece, piece)
             pltpu.make_async_remote_copy(
                 src_ref=source.at[part],
@@ -112,7 +112,6 @@
             return carry
 
         lax.fori_loop(1, CLASSES, send, 0)
-        target[0:piece, :] = source[0:piece, :]
 
     def wait_item(buffer, sem):
         part = buffer.at[pl.ds(piece, lines - piece)]
@@ -142,8 +141,10 @@
     field_copy = to_partner(v, vp, 0)
     field_copy.start()
     send_item(pk0, rv0, in_send.at[0], in_recv.at[0])
+    rv0[0:piece, :] = pk0[0:piece, :]
     pack_item(1, pk1)
     send_item(pk1, rv1, in_send.at[1], in_recv.at[1])
+    rv1[0:piece, :] = pk1[0:piece, :]
 
     u_other[...] = tables(shear_in, other, rows)[3]
     class_col, high_col, pack, unpack = tables(shear_out, own, rows)
@@ -157,7 +158,7 @@
         rh, rl = rights.at[0, item], rights.at[1, item]
         rh[pl.ds(own, rows), :], rl[pl.ds(own, rows), :] = halves(v[item])
         rh[pl.ds(other, rows), :], rl[pl.ds(other, rows), :] = halves(vp[item])
-        lh[...], ll[...] = halves(v[item] * c1[item : item + 1, :])
+        lh[...], ll[...] = halves(v[item] * c1[item, 0])
         for tile in range(columns // 256):
             span = slice(tile * 256, tile * 256 + 256)
             acc[item, :, span] = (1.0 - mixing) * v[item, :, span] + mixing * (acc[item, :, span] + ladder(tile, rh, rl))
@@ -171,7 +172,7 @@
         rh[pl.ds(own, rows), :] = product(u_own[...], high).astype(jnp.bfloat16)
         rl[pl.ds(own, rows), :] = product(u_own[...], low).astype(jnp.bfloat16)
         left = product(q_mix[...], high) + product(q_mix[...], low)
-        lh[...], ll[...] = halves(left * c2[item : item + 1, :])
+        lh[...], ll[...] = halves(left * c2[item, 0])
         copy.wait()
         high, low = plain(arrived_pair)
         rh[pl.ds(other, rows), :] = product(u_other[...], high).astype(jnp.bfloat16)
@@ -183,25 +184,40 @@
 
     crossed_item(0, rv0, rp0, ok0)
     send_item(ok0, or0, out_send.at[0], out_recv.at[0])
+    or0[0:piece, :] = ok0[0:piece, :]
     crossed_item(1, rv1, rp1, ok1)
     send_item(ok1, or1, out_send.at[1], out_recv.at[1])
-
-    def returned_item(item, arrived):
-        wait_item(arrived, out_recv.at[item])
-        high, low = plain(arrived)
-        term = mixing * (product(u_out[...], high) + product(u_out[...], low))
-        turned = turn_out[...] == 1
-        acc[item] += jnp.where(turned, 0.0, term)
-        acc[1 - item] += jnp.where(turned, term, 0.0)
-
-    returned_item(0, or0)
-    returned_item(1, or1)
-    store = pltpu.make_async_copy(acc, out_hbm, store_sem)
+    kept = pltpu.make_async_copy(ok1.at[pl.ds(0, piece)], or1.at[pl.ds(0, piece)], store_sem.at[1])
+    kept.start()
+
+    wait_item(or0, out_recv.at[0])
+    high, low = plain(or0)
+    term = mixing * (product(u_out[...], high) + product(u_out[...], low))
+    turned = turn_out[...] == 1
+    acc[0] += jnp.where(turned, 0.0, term)
+    acc[1] += jnp.where(turned, term, 0.0)
+    store = pltpu.make_async_copy(acc, acc_hbm, store_sem.at[0])
     store.start()
     for item, (first, second) in enumerate(((pk0, ok0), (pk1, ok1))):
         wait_item(first, in_send.at[item])
         wait_item(second, out_send.at[item])
     store.wait()
+    kept.wait()
+    wait_item(or1, out_recv.at[1])
+
+
+def finish(acc, arrived, u_out, turn_out, out):
+    rows, wide = out.shape[1:]
+    strips = arrived.shape[0] // rows
+    parts = [
+        halves(arrived[pl.ds(pl.program_id(0) * (wide // LANES) + strip, rows, stride=strips), :])
+        for strip in range(wide // LANES)
+    ]
+    high, low = jnp.concatenate([p[0] for p in parts], axis=1), jnp.concatenate([p[1] for p in parts], axis=1)
+    term = mixing * (product(u_out[...], high) + product(u_out[...], low))
+    turned = turn_out[...] == 1
+    out[0] = acc[0] + jnp.where(turned, term, 0.0)
+    out[1] = acc[1] + jnp.where(turned, 0.0, term)
 
 
 def body(vertex, bare_vertex, bubble_direct, bubble_crossed, shear_in, shear_out):
@@ -212,29 +228,49 @@
     anywhere = pl.BlockSpec(memory_space=pl.ANY)
     wide, real = jnp.float32, jnp.bfloat16
     dma = pltpu.SemaphoreType.DMA
-    updated = pl.pallas_call(
+    partial, arrived, order, turn = pl.pallas_call(
         kernel,
-        out_shape=jax.ShapeDtypeStruct(shape, wide),
+        out_shape=[
+            jax.ShapeDtypeStruct(shape, wide),
+            jax.ShapeDtypeStruct(lines, wide),
+            jax.ShapeDtypeStruct((rows, rows), real),
+            jax.ShapeDtypeStruct((rows, 1), jnp.int32),
+        ],
         in_specs=[anywhere, anywhere, vmem, vmem, vmem, vmem],
-        out_specs=anywhere,
+        out_specs=[anywhere, anywhere, vmem, vmem],
         scratch_shapes=[pltpu.VMEM(shape, wide)] * 3
-        + [pltpu.VMEM(lines, wide)] * 10
+        + [pltpu.VMEM(lines, wide)] * 9
         + [pltpu.VMEM((rows, columns), real)] * 2
         + [pltpu.VMEM((2, 4, columns, columns), real)]
-        + [pltpu.VMEM((rows, rows), real)] * 5
-        + [pltpu.VMEM((rows, 1), jnp.int32)] * 2
-        + [dma((2,)), dma, dma((3,)), dma((3,)), dma((2,)), dma((2,)), dma((2,)), dma((2,))],
+        + [pltpu.VMEM((rows, rows), real)] * 4
+        + [pltpu.VMEM((rows, 1), jnp.int32)]
+        + [dma((2,)), dma((2,)), dma((3,)), dma((3,)), dma((2,)), dma((2,)), dma((2,)), dma((2,))],
         compiler_params=pltpu.CompilerParams(
             collective_id=0, has_side_effects=True, vmem_limit_bytes=56 * 2**20
         ),
     )(
         vertex.reshape(shape),
         bare_vertex.reshape(shape),
-        bubble_direct.reshape(items, columns),
-        bubble_crossed.reshape(items, columns),
+        bubble_direct,
+        bubble_crossed,
         shear_in,
         shear_out,
     )
+    step = 2 * LANES
+    strip = pl.BlockSpec((items, rows, step), lambda i: (0, 0, i))
+    updated = pl.pallas_call(
+        finish,
+        grid=(columns // step,),
+        out_shape=jax.ShapeDtypeStruct(shape, wide),
+        in_specs=[
+            strip,
+            pl.BlockSpec(lines, lambda i: (0, 0)),
+            pl.BlockSpec((rows, rows), lambda i: (0, 0)),
+            pl.BlockSpec((rows, 1), lambda i: (0, 0)),
+        ],
+        out_specs=strip,
+        compiler_params=pltpu.CompilerParams(vmem_limit_bytes=60 * 2**20),
+    )(partial, arrived, order, turn)
     return updated.reshape(vertex.shape)
 
 

time: 127 us -> 123 us (0.969); the launches traced: 126 us -> 123 us
  local copies, waits for them, and re-layouts: 4.53 us -> 0 us
  Pallas kernels: 121 us -> 123 us
    unnamed x2 -> x0, local copies, waits for them, and re-layouts: 4.53 us -> none
    pallas_call x1 -> x2, Pallas kernels: 121 us -> 123 us  [the longest x1 118 us: body(): pl.pallas_call(kernel, out_shape=[jax.ShapeDtypeStruct(shape, wide), jax....]
where the time goes in v2:
time: 123 us
  Pallas kernels  123 us (100%)
    pallas_call x1, Pallas kernels, body(): pl.pallas_call(kernel, out_shape=[jax.ShapeDtypeStruct(shape, wide), jax....  118 us
    pallas_call x1, Pallas kernels, body(): pl.pallas_call(finish, grid=(columns // step,), out_shape=jax.ShapeDtypeS...  4.97 us

profile of v2, /device:TPU:6, one launch (start us, length us, event | category | flops | bytes accessed | tf_op | source)
XLA Modules:
  0.0 123.3 jit_solution(12436292007903042850)
XLA Ops:
  0.0 118.3 %shard_map.64 = (f32[2,384,768]{2,1,0:T(8,128)}, f32[2304,128]{1,0:T(8,128)}, bf16[384,384]{1,0:T(8,128)(2,1)}, s32[384,1]{1,0:T(8,128)}) custom-call(f32[2,384,768]{2,1,0:T(8,128)} %bitcast.5, f32[2,384,768]{2,1,0:T(8,128)} %bitcast.6, f32[2,1,1,768]{3,2,1,0:T(1,128)} %c1.1, f32[2,1,1,768]{3,2,1,0:T(1,128)} %c2.1, s32[2,768]{1,0:T(2,128)} %shear_in.1, ...), custom_call_target="tpu_custom_call" | custom-call | tf_op jit(solution)/shard_map/pallas_call | solution.py:231
  118.3 5.0 %shard_map.65 = f32[2,384,768]{2,1,0:T(8,128)} custom-call(f32[2,384,768]{2,1,0:T(8,128)} %get-tuple-element.9.acc, f32[2304,128]{1,0:T(8,128)} %get-tuple-element.10.arrived, bf16[384,384]{1,0:T(8,128)(2,1)} %get-tuple-element.11.u_out, s32[384,1]{1,0:T(8,128)} %get-tuple-element.12.turn_out), custom_call_target="tpu_custom_call" | custom-call | tf_op jit(solution)/shard_map/pallas_call | solution.py:261

commit v3 on v2

--- a/solution.py
+++ b/solution.py
@@ -48,10 +48,10 @@
 
 
 def kernel(
-    v_hbm, b_hbm, c1, c2, shear_in, shear_out, acc_hbm, or1, u_out, turn_out,
-    v, vp, acc, pk0, pk1, rv0, rv1, rp0, rp1, ok0, ok1, or0,
+    v_hbm, b_hbm, c1, c2, shear_in, shear_out, acc, or1, u_out, turn_out,
+    v, vp, pk0, pk1, rv0, rv1, rp0, rp1, ok0, ok1, or0,
     lh, ll, rights, p_in, u_own, u_other, q_mix, turn_in,
-    load_sem, store_sem, pair_send, pair_recv, in_send, in_recv, out_send, out_recv,
+    load_sem, pair_send, pair_recv, in_send, in_recv, out_send, out_recv,
 ):
     rows, columns = v.shape[1:]
     strips = columns // LANES
@@ -187,8 +187,7 @@
     or0[0:piece, :] = ok0[0:piece, :]
     crossed_item(1, rv1, rp1, ok1)
     send_item(ok1, or1, out_send.at[1], out_recv.at[1])
-    kept = pltpu.make_async_copy(ok1.at[pl.ds(0, piece)], or1.at[pl.ds(0, piece)], store_sem.at[1])
-    kept.start()
+    or1[0:piece, :] = ok1[0:piece, :]
 
     wait_item(or0, out_recv.at[0])
     high, low = plain(or0)
@@ -196,28 +195,28 @@
     turned = turn_out[...] == 1
     acc[0] += jnp.where(turned, 0.0, term)
     acc[1] += jnp.where(turned, term, 0.0)
-    store = pltpu.make_async_copy(acc, acc_hbm, store_sem.at[0])
-    store.start()
     for item, (first, second) in enumerate(((pk0, ok0), (pk1, ok1))):
         wait_item(first, in_send.at[item])
         wait_item(second, out_send.at[item])
-    store.wait()
-    kept.wait()
     wait_item(or1, out_recv.at[1])
 
 
-def finish(acc, arrived, u_out, turn_out, out):
-    rows, wide = out.shape[1:]
-    strips = arrived.shape[0] // rows
-    parts = [
-        halves(arrived[pl.ds(pl.program_id(0) * (wide // LANES) + strip, rows, stride=strips), :])
-        for strip in range(wide // LANES)
-    ]
-    high, low = jnp.concatenate([p[0] for p in parts], axis=1), jnp.concatenate([p[1] for p in parts], axis=1)
-    term = mixing * (product(u_out[...], high) + product(u_out[...], low))
+def finish(acc, arrived, u_out, turn_out, out_hbm, out, store_sem):
+    items, rows, columns = out.shape
+    strips = columns // LANES
     turned = turn_out[...] == 1
-    out[0] = acc[0] + jnp.where(turned, term, 0.0)
-    out[1] = acc[1] + jnp.where(turned, 0.0, term)
+    stores = []
+    for tile in range(columns // 256):
+        span = slice(tile * 256, tile * 256 + 256)
+        parts = [halves(arrived[pl.ds(2 * tile + half, rows, stride=strips), :]) for half in range(2)]
+        high, low = jnp.concatenate([p[0] for p in parts], axis=1), jnp.concatenate([p[1] for p in parts], axis=1)
+        term = mixing * (product(u_out[...], high) + product(u_out[...], low))
+        out[0, :, span] = acc[0, :, span] + jnp.where(turned, term, 0.0)
+        out[1, :, span] = acc[1, :, span] + jnp.where(turned, 0.0, term)
+        stores.append(pltpu.make_async_copy(out.at[:, :, span], out_hbm.at[:, :, span], store_sem.at[tile]))
+        stores[-1].start()
+    for store in stores:
+        store.wait()
 
 
 def body(vertex, bare_vertex, bubble_direct, bubble_crossed, shear_in, shear_out):
@@ -231,22 +230,22 @@
     partial, arrived, order, turn = pl.pallas_call(
         kernel,
         out_shape=[
-            jax.ShapeDtypeStruct(shape, wide),
-            jax.ShapeDtypeStruct(lines, wide),
-            jax.ShapeDtypeStruct((rows, rows), real),
-            jax.ShapeDtypeStruct((rows, 1), jnp.int32),
+            pltpu.VMEM(shape, wide),
+            pltpu.VMEM(lines, wide),
+            pltpu.VMEM((rows, rows), real),
+            pltpu.VMEM((rows, 1), jnp.int32),
         ],
         in_specs=[anywhere, anywhere, vmem, vmem, vmem, vmem],
-        out_specs=[anywhere, anywhere, vmem, vmem],
-        scratch_shapes=[pltpu.VMEM(shape, wide)] * 3
+        out_specs=[vmem] * 4,
+        scratch_shapes=[pltpu.VMEM(shape, wide)] * 2
         + [pltpu.VMEM(lines, wide)] * 9
         + [pltpu.VMEM((rows, columns), real)] * 2
         + [pltpu.VMEM((2, 4, columns, columns), real)]
         + [pltpu.VMEM((rows, rows), real)] * 4
         + [pltpu.VMEM((rows, 1), jnp.int32)]
-        + [dma((2,)), dma((2,)), dma((3,)), dma((3,)), dma((2,)), dma((2,)), dma((2,)), dma((2,))],
+        + [dma((2,)), dma((3,)), dma((3,)), dma((2,)), dma((2,)), dma((2,)), dma((2,))],
         compiler_params=pltpu.CompilerParams(
-            collective_id=0, has_side_effects=True, vmem_limit_bytes=56 * 2**20
+            collective_id=0, has_side_effects=True, vmem_limit_bytes=60 * 2**20
         ),
     )(
         vertex.reshape(shape),
@@ -256,20 +255,13 @@
         shear_in,
         shear_out,
     )
-    step = 2 * LANES
-    strip = pl.BlockSpec((items, rows, step), lambda i: (0, 0, i))
     updated = pl.pallas_call(
         finish,
-        grid=(columns // step,),
         out_shape=jax.ShapeDtypeStruct(shape, wide),
-        in_specs=[
-            strip,
-            pl.BlockSpec(lines, lambda i: (0, 0)),
-            pl.BlockSpec((rows, rows), lambda i: (0, 0)),
-            pl.BlockSpec((rows, 1), lambda i: (0, 0)),
-        ],
-        out_specs=strip,
-        compiler_params=pltpu.CompilerParams(vmem_limit_bytes=60 * 2**20),
+        in_specs=[vmem] * 4,
+        out_specs=anywhere,
+        scratch_shapes=[pltpu.VMEM(shape, wide), dma((columns // 256,))],
+        compiler_params=pltpu.CompilerParams(vmem_limit_bytes=16 * 2**20),
     )(partial, arrived, order, turn)
     return updated.reshape(vertex.shape)
 

time: 123 us -> 120 us (0.976)
  Pallas kernels: 123 us -> 119 us
    pallas_call x2, Pallas kernels: 123 us -> 119 us  [the longest x1 117 us: body(): pl.pallas_call(kernel, out_shape=[pltpu.VMEM(shape, wide), pltpu.VMEM(lin...]
where the time goes in v3:
time: 120 us
  Pallas kernels  119 us (99%)
    pallas_call x1, Pallas kernels, body(): pl.pallas_call(kernel, out_shape=[pltpu.VMEM(shape, wide), pltpu.VMEM(lin...  117 us

profile of v3, /device:TPU:6, one launch (start us, length us, event | category | flops | bytes accessed | tf_op | source)
XLA Modules:
  0.0 119.5 jit_solution(430932875912135168)
XLA Ops:
  0.0 117.4 %shard_map.64 = (f32[2,384,768]{2,1,0:T(8,128)S(1)}, f32[2304,128]{1,0:T(8,128)S(1)}, bf16[384,384]{1,0:T(8,128)(2,1)S(1)}, s32[384,1]{1,0:T(8,128)S(1)}) custom-call(f32[2,384,768]{2,1,0:T(8,128)} %bitcast.5, f32[2,384,768]{2,1,0:T(8,128)} %bitcast.6, f32[2,1,1,768]{3,2,1,0:T(1,128)} %c1.1, f32[2,1,1,768]{3,2,1,0:T(1,128)} %c2.1, s32[2,768]{1,0:T(2,128)} %shear_in.1, ...), custom_call_target="tpu_custom_call" | custom-call | tf_op jit(solution)/shard_map/pallas_call | solution.py:230
  117.5 1.9 %shard_map.65 = f32[2,384,768]{2,1,0:T(8,128)} custom-call(f32[2,384,768]{2,1,0:T(8,128)S(1)} %get-tuple-element.9.acc, f32[2304,128]{1,0:T(8,128)S(1)} %get-tuple-element.10.arrived, bf16[384,384]{1,0:T(8,128)(2,1)S(1)} %get-tuple-element.11.u_out, s32[384,1]{1,0:T(8,128)S(1)} %get-tuple-element.12.turn_out), custom_call_target="tpu_custom_call" | custom-call | tf_op jit(solution)/shard_map/pallas_call | solution.py:258

commit v4 on v3

--- a/solution.py
+++ b/solution.py
@@ -138,30 +138,19 @@
     pack_item(0, pk0)
     pl.semaphore_wait(barrier, CLASSES)
 
-    field_copy = to_partner(v, vp, 0)
-    field_copy.start()
     send_item(pk0, rv0, in_send.at[0], in_recv.at[0])
     rv0[0:piece, :] = pk0[0:piece, :]
     pack_item(1, pk1)
     send_item(pk1, rv1, in_send.at[1], in_recv.at[1])
     rv1[0:piece, :] = pk1[0:piece, :]
+    field_copy = to_partner(v, vp, 0)
+    field_copy.start()
 
     u_other[...] = tables(shear_in, other, rows)[3]
     class_col, high_col, pack, unpack = tables(shear_out, own, rows)
     turn_out[...] = (high_col + (class_col > kx).astype(jnp.int32)) & 1
     u_out[...] = unpack
     q_mix[...] = product(pack, u_own[...]).astype(jnp.bfloat16)
-
-    loads[1].wait()
-    field_copy.wait()
-    for item in range(2):
-        rh, rl = rights.at[0, item], rights.at[1, item]
-        rh[pl.ds(own, rows), :], rl[pl.ds(own, rows), :] = halves(v[item])
-        rh[pl.ds(other, rows), :], rl[pl.ds(other, rows), :] = halves(vp[item])
-        lh[...], ll[...] = halves(v[item] * c1[item, 0])
-        for tile in range(columns // 256):
-            span = slice(tile * 256, tile * 256 + 256)
-            acc[item, :, span] = (1.0 - mixing) * v[item, :, span] + mixing * (acc[item, :, span] + ladder(tile, rh, rl))
 
     def crossed_item(item, arrived, arrived_pair, into):
         rh, rl = rights.at[0, 2 + item], rights.at[1, 2 + item]
@@ -188,6 +177,17 @@
     crossed_item(1, rv1, rp1, ok1)
     send_item(ok1, or1, out_send.at[1], out_recv.at[1])
     or1[0:piece, :] = ok1[0:piece, :]
+
+    loads[1].wait()
+    field_copy.wait()
+    for item in range(2):
+        rh, rl = rights.at[0, item], rights.at[1, item]
+        rh[pl.ds(own, rows), :], rl[pl.ds(own, rows), :] = halves(v[item])
+        rh[pl.ds(other, rows), :], rl[pl.ds(other, rows), :] = halves(vp[item])
+        lh[...], ll[...] = halves(v[item] * c1[item, 0])
+        for tile in range(columns // 256):
+            span = slice(tile * 256, tile * 256 + 256)
+            acc[item, :, span] = (1.0 - mixing) * v[item, :, span] + mixing * (acc[item, :, span] + ladder(tile, rh, rl))
 
     wait_item(or0, out_recv.at[0])
     high, low = plain(or0)

time: 120 us -> 120 us (level)
  no operation moved by 1% of the time
where the time goes in v4:
time: 120 us
  Pallas kernels  119 us (99%)
    pallas_call x1, Pallas kernels, body(): pl.pallas_call(kernel, out_shape=[pltpu.VMEM(shape, wide), pltpu.VMEM(lin...  117 us

profile of v4, /device:TPU:6, one launch (start us, length us, event | category | flops | bytes accessed | tf_op | source)
XLA Modules:
  0.0 119.5 jit_solution(13762161212576087446)
XLA Ops:
  0.0 117.4 %shard_map.64 = (f32[2,384,768]{2,1,0:T(8,128)S(1)}, f32[2304,128]{1,0:T(8,128)S(1)}, bf16[384,384]{1,0:T(8,128)(2,1)S(1)}, s32[384,1]{1,0:T(8,128)S(1)}) custom-call(f32[2,384,768]{2,1,0:T(8,128)} %bitcast.5, f32[2,384,768]{2,1,0:T(8,128)} %bitcast.6, f32[2,1,1,768]{3,2,1,0:T(1,128)} %c1.1, f32[2,1,1,768]{3,2,1,0:T(1,128)} %c2.1, s32[2,768]{1,0:T(2,128)} %shear_in.1, ...), custom_call_target="tpu_custom_call" | custom-call | tf_op jit(solution)/shard_map/pallas_call | solution.py:230
  117.5 1.9 %shard_map.65 = f32[2,384,768]{2,1,0:T(8,128)} custom-call(f32[2,384,768]{2,1,0:T(8,128)S(1)} %get-tuple-element.9.acc, f32[2304,128]{1,0:T(8,128)S(1)} %get-tuple-element.10.arrived, bf16[384,384]{1,0:T(8,128)(2,1)S(1)} %get-tuple-element.11.u_out, s32[384,1]{1,0:T(8,128)S(1)} %get-tuple-element.12.turn_out), custom_call_target="tpu_custom_call" | custom-call | tf_op jit(solution)/shard_map/pallas_call | solution.py:258

commit v5 on v4

--- a/solution.py
+++ b/solution.py
@@ -67,6 +67,16 @@
         tx, ty, tz = (x + (step >> 5)) & 3, (y + (step >> 3)) & 3, (z + step) & 7
         return (tz >> 2) * NX + tx, (tz & 3) * NY + ty
 
+    def each_place(visit):
+        def plane(at, carry):
+            for step in range(NZ):
+                visit(at * NZ + step, carry)
+            return carry
+
+        for step in range(1, NZ):
+            visit(step, 0)
+        lax.fori_loop(1, NX * NY, plane, 0)
+
     loads = [pltpu.make_async_copy(v_hbm, v, load_sem.at[0]), pltpu.make_async_copy(b_hbm, acc, load_sem.at[1])]
     for load in loads:
         load.start()
@@ -78,7 +88,7 @@
         pl.semaphore_signal(barrier, inc=1, device_id=(tx, ty, af), device_id_type=MESH)
         return carry
 
-    lax.fori_loop(1, CLASSES, greet, 0)
+    each_place(greet)
     pl.semaphore_signal(barrier, inc=1, device_id=partner, device_id_type=MESH)
 
     class_col, high_col, pack, unpack = tables(shear_in, own, rows)
@@ -111,7 +121,7 @@
             ).start()
             return carry
 
-        lax.fori_loop(1, CLASSES, send, 0)
+        each_place(send)
 
     def wait_item(buffer, sem):
         part = buffer.at[pl.ds(piece, lines - piece)]

time: 120 us -> 119 us (level)
  no operation moved by 1% of the time
where the time goes in v5:
time: 119 us
  Pallas kernels  119 us (100%)
    pallas_call x1, Pallas kernels, body(): pl.pallas_call(kernel, out_shape=[pltpu.VMEM(shape, wide), pltpu.VMEM(lin...  117 us

profile of v5, /device:TPU:6, one launch (start us, length us, event | category | flops | bytes accessed | tf_op | source)
XLA Modules:
  0.0 119.2 jit_solution(5704344558407170941)
XLA Ops:
  0.0 117.1 %shard_map.64 = (f32[2,384,768]{2,1,0:T(8,128)S(1)}, f32[2304,128]{1,0:T(8,128)S(1)}, bf16[384,384]{1,0:T(8,128)(2,1)S(1)}, s32[384,1]{1,0:T(8,128)S(1)}) custom-call(f32[2,384,768]{2,1,0:T(8,128)} %bitcast.5, f32[2,384,768]{2,1,0:T(8,128)} %bitcast.6, f32[2,1,1,768]{3,2,1,0:T(1,128)} %c1.1, f32[2,1,1,768]{3,2,1,0:T(1,128)} %c2.1, s32[2,768]{1,0:T(2,128)} %shear_in.1, ...), custom_call_target="tpu_custom_call" | custom-call | tf_op jit(solution)/shard_map/pallas_call | solution.py:240
  117.1 1.9 %shard_map.65 = f32[2,384,768]{2,1,0:T(8,128)} custom-call(f32[2,384,768]{2,1,0:T(8,128)S(1)} %get-tuple-element.9.acc, f32[2304,128]{1,0:T(8,128)S(1)} %get-tuple-element.10.arrived, bf16[384,384]{1,0:T(8,128)(2,1)S(1)} %get-tuple-element.11.u_out, s32[384,1]{1,0:T(8,128)S(1)} %get-tuple-element.12.turn_out), custom_call_target="tpu_custom_call" | custom-call | tf_op jit(solution)/shard_map/pallas_call | solution.py:268
